TPU v7x, 512 devices: a whole 4x8x8 slice. The times are simulated.
512 devices in a mesh: blk: 128 (over x, y, z_hi, core), hid: 4 (over z_lo).
Axes of the slice: x: 4, y: 8, z: 8 (z_hi: 2, z_lo: 4; z = z_hi * 4 + z_lo), core: 2. Of those that a mesh axis runs over, the one named last changes fastest.
Arguments:
- out_grad: bfloat16 [16384, 2048], P('blk', 'hid'), may hold values from -6 to 6
- hidden: bfloat16 [16384, 8, 1536], P('blk', None, 'hid'), may hold values from -0.796875 to 0.796875
- gates: float32 [16384, 8], P('blk'), may hold values from 0.05 to 0.6
- expert_ids: int32 [16384, 8], P('blk'), may hold values from 0 to 127, all different within a row; in each aligned block of 128 rows (0 to 127, 128 to 255, ...) at most 12 rows name the same one
- down_weight: bfloat16 [128, 1536, 2048], P('blk', 'hid'), may hold values from -0.15625 to 0.15625
Outputs:
- weight_grad: bfloat16 [128, 1536, 2048], P('blk', 'hid')
- hidden_grad: bfloat16 [16384, 8, 1536], P('blk', None, 'hid')
- gate_grad: float32 [16384, 8], P('blk')
Inputs may be any that keep to these rules, and one draw needn't show every extreme that they name: `expert_ids`: each row names 8 different experts; among the rows of one index of blk no expert is named more than 12 times, a bound that some block reaches.
All inputs are finite; a program needn't handle non-finite values.
Results may differ from a plain program's by a relative error of at most 0.0049.
Values may be sent and summed in bfloat16 or wider, within the bound.
A program may use at most 128 MiB of HBM per device.

v0:
```python
import jax
import jax.numpy as jnp
from jax import lax
from jax.sharding import PartitionSpec as P


def shards(out_grad, hidden, gates, expert_ids, down_weight):
    token_count = expert_ids.shape[0]
    top_count = expert_ids.shape[1]
    unit_count = hidden.shape[2]
    experts = lax.axis_size("blk")
    capacity = min(token_count, 3 * token_count * top_count // (2 * experts))
    slot_count = token_count * top_count
    flat_ids = expert_ids.reshape(slot_count)
    onehot = (flat_ids[:, None] == jnp.arange(experts, dtype=jnp.int32)[None, :]).astype(jnp.int32)
    slot_rank = jnp.sum(onehot * (jnp.cumsum(onehot, axis=0) - 1), axis=1)
    target = flat_ids * capacity + slot_rank
    slot_table = jnp.full((experts * capacity,), slot_count, jnp.int32)
    slot_table = slot_table.at[target].set(jnp.arange(slot_count, dtype=jnp.int32))
    filled = slot_table < slot_count
    source = jnp.minimum(slot_table, slot_count - 1)
    token_of = source // top_count
    weighted = (gates[:, :, None] * hidden.astype(jnp.float32)).astype(jnp.bfloat16)
    weighted = weighted.reshape(slot_count, unit_count)
    send_hidden = jnp.where(filled[:, None], weighted[source], jnp.zeros((), jnp.bfloat16))
    send_hidden = send_hidden.reshape(experts, capacity, unit_count)
    full_rows = lax.all_gather(out_grad, "hid", axis=1, tiled=True)
    send_grads = jnp.where(filled[:, None], full_rows[token_of], jnp.zeros((), jnp.bfloat16))
    send_grads = send_grads.reshape(experts, capacity, full_rows.shape[1])
    recv_grads, recv_hidden = (
        lax.all_to_all(send_grads, "blk", split_axis=0, concat_axis=0, tiled=True),
        lax.all_to_all(send_hidden, "blk", split_axis=0, concat_axis=0, tiled=True),
    )
    expert_rows = recv_grads.reshape(experts * capacity, recv_grads.shape[2])
    hidden_rows = recv_hidden.reshape(experts * capacity, unit_count)
    weight = down_weight[0]
    pre_grad = lax.dot_general(
        expert_rows, weight, (((1,), (1,)), ((), ())), preferred_element_type=jnp.float32
    ).astype(jnp.bfloat16)
    weight_grad = lax.dot_general(
        hidden_rows, expert_rows, (((0,), (0,)), ((), ())), preferred_element_type=jnp.float32
    ).astype(jnp.bfloat16)
    returned = lax.all_to_all(
        pre_grad.reshape(experts, capacity, unit_count),
        "blk",
        split_axis=0,
        concat_axis=0,
        tiled=True,
    )
    slot_grads = returned.reshape(experts * capacity, unit_count)[target]
    slot_grads = slot_grads.reshape(token_count, top_count, unit_count).astype(jnp.float32)
    hidden_grad = (gates[:, :, None] * slot_grads).astype(jnp.bfloat16)
    partial_value = jnp.sum(hidden.astype(jnp.float32) * slot_grads, axis=-1)
    gate_grad = lax.psum(partial_value, "hid")
    return (weight_grad[None], hidden_grad, gate_grad)


def solution(mesh):
    placed = (
        P("blk", "hid"),
        P("blk", None, "hid"),
        P("blk", None),
        P("blk", None),
        P("blk", "hid", None),
    )
    return jax.shard_map(
        shards,
        mesh=mesh,
        in_specs=placed,
        out_specs=(P("blk", "hid", None), P("blk", None, "hid"), P("blk", None)),
        check_vma=False,
    )
```

profile of v0, /device:TPU:1, one launch (start us, length us, event | category | flops | bytes accessed | tf_op | source)
XLA Modules:
  0.0 414.7 jit_solution(12069853088663524616)
XLA Ops:
  0.6 0.9 copy.21
  1.7 0.7 broadcast_multiply_fusion
  2.5 0.2 fusion.14
  2.8 0.1 copy.24
  2.9 0.1 copy.20
  3.1 0.4 fusion.13
  3.5 4.3 %scatter_custom_fusion = s32[1536]{0:T(1024)S(1)} fusion(s32[1024]{0:T(1024)S(1)} %bitcast.27, s32[1024]{0:T(1024)S(1)} %iota.11, s32[]{:T(128)} %constant.12.clone.1), kind=kCustom, calls=%fused_computation.42 | custom fusion | bytes 6148 | tf_op jit(solution)/shard_map/scatter | solution.py:19
  7.9 17.7 %all_gather.3 = bf16[128,2048]{1,0:T(8,128)(2,1)S(1)} all-gather(bf16[128,512]{1,0:T(8,128)(2,1)S(1)} %copy-done.2), channel_id=1, replica_groups=mesh['blk'=128,'hid'=4] {'hid'}, dimensions={1}, use_global_device_ids=true | all-gather | bytes 655360 | tf_op jit(solution)/shard_map/all_gather | solution.py:27
  25.7 7.1 %gather_fusion.1 = bf16[1536,2048]{1,0:T(8,128)(2,1)} fusion(bf16[128,2048]{1,0:T(8,128)(2,1)S(1)} %all_gather.3, s32[2048]{0:T(1024)S(1)} %pad_clamp_fusion), kind=kCustom, calls=%fused_computation.1 | custom fusion | bytes 12589056 | tf_op jit(solution)/shard_map/gather | solution.py:28
  32.7 10.6 %gather.16 = bf16[128,12,2048]{2,1,0:T(8,128)(2,1)} reshape(bf16[1536,2048]{1,0:T(8,128)(2,1)} %gather_fusion.1) | data formatting | bytes 12582912 | tf_op jit(solution)/shard_map/gather | solution.py:28
  43.3 0.1 broadcast_in_dim.42
  43.4 7.3 %broadcast_select_fusion = bf16[128,12,2048]{2,1,0:T(8,128)(2,1)} fusion(bf16[128,12,2048]{2,1,0:T(8,128)(2,1)} %gather.16, pred[128,12]{1,0:T(8,128)(4,1)S(1)} %broadcast_in_dim.42), kind=kLoop, calls=%fused_computation.4 | loop fusion | flops 3145728 | bytes 12584448 | tf_op jit(solution)/shard_map/jit(_where)/select_n | solution.py:28
  50.7 207.1 %all_to_all.15 = bf16[128,12,2048]{2,1,0:T(8,128)(2,1)} all-to-all(bf16[128,12,2048]{2,1,0:T(8,128)(2,1)} %broadcast_select_fusion), channel_id=1, replica_groups=mesh['blk'=128,'hid'=4] {'blk'}, dimensions={0} | all-to-all | bytes 12582912 | tf_op jit(solution)/shard_map/all_to_all | solution.py:31
  257.8 10.7 %reshape.87 = bf16[1536,2048]{1,0:T(8,128)(2,1)} reshape(bf16[128,12,2048]{2,1,0:T(8,128)(2,1)} %all_to_all.15) | data formatting | bytes 12582912 | tf_op jit(solution)/shard_map/reshape | solution.py:34
  268.5 6.2 %convolution_convert_fusion = bf16[1536,384]{1,0:T(8,128)(2,1)S(1)} fusion(bf16[1536,2048]{1,0:T(8,128)(2,1)} %reshape.87, bf16[1,384,2048]{2,1,0:T(8,128)(2,1)S(1)} %copy-done), kind=kOutput, calls=%fused_computation.8 | convolution fusion | flops 2416508928 | bytes 9043968 | tf_op jit(solution)/shard_map/dot_general | solution.py:37
  274.7 1.3 reshape.88
  276.0 13.0 %all-to-all-start.2 = ((bf16[128,12,384]{2,1,0:T(8,128)(2,1)}), bf16[128,12,384]{2,1,0:T(8,128)(2,1)}, u32[]{:S(2)}, u32[]{:S(2)}) async-start(bf16[128,12,384]{2,1,0:T(8,128)(2,1)} %reshape.88), calls=%async_computation.2 | async-start | bytes 3145728 | tf_op jit(solution)/shard_map/all_to_all | solution.py:43
  289.0 0.7 copy.25
  289.7 0.6 pad_clamp_fusion.1
  290.3 0.6 broadcast_clamp_fusion
  290.9 40.5 %all-to-all-done.2 = bf16[128,12,384]{2,1,0:T(8,128)(2,1)} async-done(((bf16[128,12,384]{2,1,0:T(8,128)(2,1)}), bf16[128,12,384]{2,1,0:T(8,128)(2,1)}, u32[]{:S(2)}, u32[]{:S(2)}) %all-to-all-start.2) | async-done | bytes 1179680 | tf_op jit(solution)/shard_map/all_to_all | solution.py:43
  331.4 2.3 reshape.89
  333.7 4.4 %gather_fusion.2 = bf16[1024,384]{1,0:T(8,128)(2,1)S(1)} fusion(bf16[1536,384]{1,0:T(8,128)(2,1)S(1)} %reshape.89, s32[1024]{0:T(1024)} %broadcast_clamp_fusion), kind=kCustom, calls=%fused_computation.2 | custom fusion | bytes 1576960 | tf_op jit(solution)/shard_map/gather | solution.py:50
  338.1 3.1 fusion.9
  341.3 5.3 %gather_fusion = bf16[1536,384]{1,0:T(8,128)(2,1)} fusion(bf16[1024,384]{1,0:T(8,128)(2,1)S(1)} %get-tuple-element.8, s32[2048]{0:T(1024)S(1)} %copy-done.3), kind=kCustom, calls=%fused_computation | custom fusion | bytes 2365440 | tf_op jit(solution)/shard_map/gather | solution.py:25
  346.6 2.2 gather.14
  348.7 1.4 broadcast_select_fusion.1
  350.1 9.0 %all-to-all-start = ((bf16[128,12,384]{2,1,0:T(8,128)(2,1)}), bf16[128,12,384]{2,1,0:T(8,128)(2,1)S(1)}, u32[]{:S(2)}, u32[]{:S(2)}) async-start(bf16[128,12,384]{2,1,0:T(8,128)(2,1)} %broadcast_select_fusion.1), calls=%async_computation | async-start | bytes 3145728 | tf_op jit(solution)/shard_map/all_to_all | solution.py:32
  359.1 38.7 %psum.7 = f32[128,8]{1,0:T(8,128)S(1)} all-reduce(f32[128,8]{1,0:T(8,128)S(1)} %copy-done.1), channel_id=1, replica_groups=mesh['blk'=128,'hid'=4] {'hid'}, use_global_device_ids=true, to_apply=%region_5.6 | all-reduce | flops 1024 | bytes 8192 | tf_op jit(solution)/shard_map/psum | solution.py:54
  397.8 0.7 copy.28
  398.5 3.4 all-to-all-done
  401.9 12.8 %fusion.4 = bf16[1,384,2048]{2,1,0:T(8,128)(2,1)} fusion(bf16[128,12,2048]{2,1,0:T(8,128)(2,1)} %all_to_all.15, bf16[128,12,384]{2,1,0:T(8,128)(2,1)S(1)} %all-to-all-done), kind=kOutput, calls=%fused_computation.9 | convolution fusion | flops 2416705536 | bytes 9043968 | tf_op jit(solution)/shard_map/dot_general | solution.py:40
  (23 shorter events, 0.5 us)
Async XLA Ops:
  0.6 267.8 %copy-start = (bf16[1,384,2048]{2,1,0:T(8,128)(2,1)S(1)}, bf16[1,384,2048]{2,1,0:T(8,128)(2,1)}, u32[]{:S(2)}) copy-start(bf16[1,384,2048]{2,1,0:T(8,128)(2,1)} %param.9) | copy-start | bytes 4718596
  2.7 5.2 %copy-start.2 = (bf16[128,512]{1,0:T(8,128)(2,1)S(1)}, bf16[128,512]{1,0:T(8,128)(2,1)}, u32[]{:S(2)}) copy-start(bf16[128,512]{1,0:T(8,128)(2,1)} %param.5) | copy-start | bytes 393220
  276.0 13.0 %copy-start.4 = (f32[128,8]{0,1:T(8,128)S(1)}, f32[128,8]{0,1:T(8,128)}, u32[]{:S(2)}) copy-start(f32[128,8]{0,1:T(8,128)} %param.7) | copy-start | bytes 12292
  276.0 55.4 %all-to-all-start.2 = ((bf16[128,12,384]{2,1,0:T(8,128)(2,1)}), bf16[128,12,384]{2,1,0:T(8,128)(2,1)}, u32[]{:S(2)}, u32[]{:S(2)}) async-start(bf16[128,12,384]{2,1,0:T(8,128)(2,1)} %reshape.88), calls=%async_computation.2 | async-start | bytes 3145728 | tf_op jit(solution)/shard_map/all_to_all | solution.py:43
  338.1 3.2 copy-start.3
  350.1 9.0 %copy-start.1 = (f32[128,8]{1,0:T(8,128)S(1)}, f32[128,8]{1,0:T(8,128)}, u32[]{:S(2)}) copy-start(f32[128,8]{1,0:T(8,128)} %get-tuple-element.6) | copy-start | bytes 12292
  350.1 51.8 %all-to-all-start = ((bf16[128,12,384]{2,1,0:T(8,128)(2,1)}), bf16[128,12,384]{2,1,0:T(8,128)(2,1)S(1)}, u32[]{:S(2)}, u32[]{:S(2)}) async-start(bf16[128,12,384]{2,1,0:T(8,128)(2,1)} %broadcast_select_fusion.1), calls=%async_computation | async-start | bytes 3145728 | tf_op jit(solution)/shard_map/all_to_all | solution.py:32
where the time goes:
time: 421 us; the launch traced here: 415 us
  blocking collectives  263 us (62%)
  local copies, waits for them, and re-layouts  51.1 us (12%)
  waiting for transfers between devices  44 us (10%)
  starting transfers between devices  22 us (5%)
  matrix products  19.1 us (5%)
  other arithmetic  14.3 us (3%)
    all_to_all x1, blocking collectives, shards(): lax.all_to_all(send_grads, 'blk', split_axis=0, concat_axis=0, tiled=True)  207 us
    all_to_all x1, waiting for transfers between devices, shards(): lax.all_to_all(pre_grad.reshape(experts, capacity, unit_count), 'blk', sp...  40.5 us
    psum x1, blocking collectives, shards(): gate_grad = lax.psum(partial_value, 'hid')  38.7 us
    all_gather x1, blocking collectives, shards(): full_rows = lax.all_gather(out_grad, 'hid', axis=1, tiled=True)  17.7 us
    gather x2, local copies, waits for them, and re-layouts, shards(): full_rows[token_of]  17.7 us
    all_to_all x1, starting transfers between devices, shards(): lax.all_to_all(pre_grad.reshape(experts, capacity, unit_count), 'blk', sp...  13 us
    dot_general x1, matrix products, shards(): lax.dot_general(hidden_rows, expert_rows, (((0,), (0,)), ((), ())), prefe...  12.8 us
    reshape x1, local copies, waits for them, and re-layouts, shards(): expert_rows = recv_grads.reshape(experts * capacity, recv_grads.shape[2])  10.7 us
  transfers between devices with their start and end apart: 2, of which 2 were waited for; matrix products, arithmetic and copies ran while one was open for 1% of the time, Pallas kernels for 0%

commit v1 on v0

v1 whole, which is shorter than its diff:
```python
import functools

import jax
import jax.numpy as jnp
import numpy as np
from jax import lax
from jax.experimental import pallas as pl
from jax.experimental.pallas import tpu as pltpu
from jax.sharding import PartitionSpec as P

MESH = pl.DeviceIdType.MESH
BF = jnp.bfloat16
F32 = jnp.float32
NX, NY, NZ, NC = 4, 8, 8, 2
QUAD = 4
CAP = 12
GRP = QUAD * CAP
TOK = 128
LANE = 128
CHUNK = QUAD * TOK
CHUNK_ROWS = CHUNK + 4 * 8
COL = NY * GRP
NQ = NY * QUAD
UNITS = 384
FEATS = 2048
SLOTS = 1024


def dot(a, b):
    return jnp.dot(a, b, preferred_element_type=F32)


def dot_nt(a, b):
    return lax.dot_general(a, b, (((1,), (1,)), ((), ())), preferred_element_type=F32)


def dot_tn(a, b):
    return lax.dot_general(a, b, (((0,), (0,)), ((), ())), preferred_element_type=F32)


def kernel(
    og, ids16, weighted, hidden, tgt_row, tgt_col, perm, weight,
    slot_grads, gate_out, weight_grad,
    stage, ex, cols, gsel, sendx, recvx, rows,
    hs, hx, hq_send, hq, hrows,
    rq_send, rq, r2, rx, undo, w_vmem, wg_vmem, gate_recv,
    ex_s, ex_r, ra_s, ra_r, rb_s, rb_r, x_s, x_r,
    hx_s, hx_r, hq_s, hq_r, rq_s, rq_r, rx_s, rx_r, gt_s, gt_r, w_sem, o_sem,
):
    blk = lax.axis_index("blk")
    hid = lax.axis_index("hid")
    x = blk // 32
    y = (blk // 4) % 8
    zhi = (blk // 2) % 2
    core = blk % 2
    z = zhi * 4 + hid
    quad = zhi * 2 + core
    q = blk % 32

    def dev(x_, y_, z_, c_):
        return (x_ * 32 + y_ * 4 + (z_ // 4) * 2 + c_, z_ % 4)

    def dev_q(q_):
        return (x * 32 + q_, hid)

    def remote(src, dst, send_sem, recv_sem, device):
        copy = pltpu.make_async_remote_copy(
            src_ref=src, dst_ref=dst, send_sem=send_sem, recv_sem=recv_sem,
            device_id=device, device_id_type=MESH,
        )
        copy.start()

    def wait_for(ref, sem):
        pltpu.make_async_copy(ref, ref, sem).wait()

    pa = core * y + (1 - core) * z
    pb = core * z + (1 - core) * y

    def dev_ab(a, b):
        return dev(x, core * a + (1 - core) * b, core * b + (1 - core) * a, core)

    barrier = pltpu.get_barrier_semaphore()

    def greet(device):
        pl.semaphore_signal(barrier, inc=1, device_id=device, device_id_type=MESH)

    greeted = 0
    for step in (1, 7):
        greet(dev_ab((pa + step) % 8, pb))
        greet(dev_ab(pa, (pb + step) % 8))
        greeted += 2
    for d in range(1, 8):
        greet(dev((x + d // 2) % 4, y, z, (core + d % 2) % 2))
        greeted += 1
    for d in range(1, 4):
        greet((blk, (hid + d) % 4))
        greeted += 1

    def greet_q(d, c):
        greet(dev_q((q + d) % 32))
        return c

    lax.fori_loop(1, 32, greet_q, 0)
    greeted += 31

    def feature_block(c, z_):
        return (z_ % 4) * 512 + (z_ // 4) * 256 + c * 128

    for c in range(2):
        for z_ in range(8):
            pltpu.make_async_copy(
                weight.at[0, :, pl.ds(feature_block(c, z_), LANE)],
                w_vmem.at[:, pl.ds((c * 8 + z_) * LANE, LANE)],
                w_sem,
            ).start()

    for j in range(QUAD):
        stage[j, 0:TOK, :] = og[:, j * LANE:(j + 1) * LANE]
        stage[j, TOK:TOK + 16, :] = ids16[...]

    pl.semaphore_wait(barrier, greeted)

    for d in range(1, 4):
        other = (quad + d) % 4
        remote(
            stage.at[other], ex.at[quad], ex_s, ex_r.at[d],
            dev(x, y, (other // 2) * 4 + hid, other % 2),
        )
    ex[quad] = stage[quad]

    def select_hidden(dx):
        xd = (x + dx) % 4
        at = lax.broadcasted_iota(jnp.int32, (COL, SLOTS), 0) + xd * COL
        pick = jnp.where(at == tgt_row[...], 1.0, 0.0).astype(BF)
        picked = dot(pick, weighted[...]).astype(BF)
        if dx == 0:
            hx[x] = picked
        else:
            hs[dx] = picked
            remote(
                hs.at[dx], hx.at[x], hx_s, hx_r.at[dx],
                dev(xd, y, z, core),
            )

    for dx in (2, 1, 3, 0):
        select_hidden(dx)

    for d in range(1, 4):
        wait_for(ex.at[0], ex_r.at[d])
    own = cols.at[pb, pa]
    for j in range(QUAD):
        own[j * TOK:(j + 1) * TOK, :] = ex[j, 0:TOK, :]
    own[CHUNK:CHUNK_ROWS, :] = jnp.concatenate(
        [ex[j, TOK:TOK + 16, :].astype(F32)[0:8] for j in range(QUAD)], axis=0
    ).astype(BF)

    half_rows = CHUNK_ROWS // 2
    for step in range(1, 5):
        for way, sign in ((0, 1), (1, -1)):
            a = (pa - sign * (step - 1)) % 8
            if step > 1:
                wait_for(cols.at[0, 0], ra_r.at[way, step - 1])
            ref = cols.at[pb, a]
            if step == 4:
                ref = cols.at[pb, a, pl.ds(way * half_rows, half_rows)]
            remote(ref, ref, ra_s, ra_r.at[way, step], dev_ab((pa + sign) % 8, pb))
    for way in range(2):
        wait_for(cols.at[0, 0, pl.ds(0, half_rows)], ra_r.at[way, 4])

    def ring_wait(step):
        for way in range(2):
            for piece in range(2):
                if step < 4 or piece == way:
                    wait_for(cols.at[0, pl.ds(0, 4)], rb_r.at[way, step, piece])

    def ring_send(step):
        for way, sign in ((0, 1), (1, -1)):
            b = (pb - sign * (step - 1)) % 8
            for piece in range(2):
                if step > 1:
                    wait_for(cols.at[0, pl.ds(0, 4)], rb_r.at[way, step - 1, piece])
                if step < 4 or piece == way:
                    ref = cols.at[b, pl.ds(4 * piece, 4)]
                    remote(
                        ref, ref, rb_s, rb_r.at[way, step, piece],
                        dev_ab(pa, (pb + sign) % 8),
                    )

    before = jnp.where(
        lax.broadcasted_iota(jnp.int32, (TOK, TOK), 0)
        < lax.broadcasted_iota(jnp.int32, (TOK, TOK), 1), 1.0, 0.0,
    ).astype(BF)
    which = lax.broadcasted_iota(jnp.int32, (8, TOK), 0)
    wanted = (
        ((x + which // 2) % 4) * 32 + y * 4 + zhi * 2 + (core + which % 2) % 2
    ).astype(F32)

    def make_pick(col, a, b):
        ids = cols[b, a, CHUNK:CHUNK_ROWS, :].astype(F32)
        found = []
        for j in range(QUAD):
            hit = jnp.zeros((8, TOK), F32)
            for k in range(8):
                row = ids[j * 8 + k:j * 8 + k + 1, :]
                hit = hit + jnp.where(row == wanted, 1.0, 0.0)
            found.append(hit)
        rank = dot(jnp.concatenate(found, axis=0).astype(BF), before)
        code = jnp.concatenate(
            [
                jnp.where(found[j] > 0.5, rank[j * 8:(j + 1) * 8] + float(CAP * j), -1.0)
                for j in range(QUAD)
            ],
            axis=1,
        )
        at = lax.broadcasted_iota(jnp.int32, (GRP, CHUNK), 0).astype(F32)
        for e in range(8):
            gsel[col, e * GRP:(e + 1) * GRP, :] = jnp.where(
                at == code[e:e + 1, :], 1.0, 0.0
            ).astype(BF)

    def select(b, first):
        @pl.when(core == 0)
        def _():
            make_pick(b, 0, b)

        if first:
            @pl.when(core == 1)
            def _():
                def one(a, c):
                    make_pick(a, a, b)
                    return c

                lax.fori_loop(0, 8, one, 0)

        def one_chunk(a, c):
            col = core * a + (1 - core) * b
            out = dot(gsel[col], cols[b, a, 0:CHUNK, :]).astype(BF)
            place = pl.ds(pl.multiple_of(a * GRP, GRP), GRP)
            recvx[core, x, b, place, :] = out[0:GRP]
            for e in range(1, 8):
                sendx[b, e, place, :] = out[e * GRP:(e + 1) * GRP]
            return c

        lax.fori_loop(0, 8, one_chunk, 0)
        for e in (4, 5, 2, 3, 6, 7, 1):
            remote(
                sendx.at[b, e], recvx.at[core, x, b], x_s, x_r.at[e // 2],
                dev((x + e // 2) % 4, y, z, (core + e % 2) % 2),
            )

    ring_send(1)
    select(pb, True)
    ring_send(2)
    select((pb - 1) % 8, False)
    select((pb + 1) % 8, False)

    for dx in range(1, 4):
        wait_for(hx.at[0], hx_r.at[dx])
    swap = perm[...]

    def relay_hidden(g, c):
        block = jnp.concatenate(
            [hx[xs, pl.ds(pl.multiple_of(g * GRP, GRP), GRP), :] for xs in range(4)],
            axis=0,
        )
        out = dot(swap, block).astype(BF)
        for j in range(4):
            hq_send[g * 4 + j] = out[j * GRP:(j + 1) * GRP]
        return c

    lax.fori_loop(0, 8, relay_hidden, 0)
    hq[q] = hq_send[q]

    def send_hidden(d, c):
        qd = (q + d) % 32
        remote(hq_send.at[qd], hq.at[q], hq_s, hq_r, dev_q(qd))
        return c

    lax.fori_loop(1, 32, send_hidden, 0)

    ring_send(3)
    select((pb - 2) % 8, False)
    select((pb + 2) % 8, False)
    ring_send(4)
    select((pb - 3) % 8, False)
    select((pb + 3) % 8, False)
    ring_wait(4)
    select((pb + 4) % 8, False)

    wait_for(w_vmem, w_sem)
    for dx in (0, 1, 3, 2):
        xs = (x - dx) % 4
        if dx == 0:
            wait_for(recvx.at[0, 0], x_r.at[0])
        else:
            wait_for(recvx.at[:, 0], x_r.at[dx])
        place = pl.ds(pl.multiple_of(xs * COL, COL), COL)
        for a in range(8):
            rows[place, a * LANE:(a + 1) * LANE] = recvx[
                0, xs, :, a * GRP:(a + 1) * GRP, :
            ].reshape(COL, LANE)
            rows[place, FEATS // 2 + a * LANE:FEATS // 2 + (a + 1) * LANE] = recvx[
                1, xs, a
            ]
        hrows[place, :] = dot_nt(rows[place, :], w_vmem[...]).astype(BF)

    def return_group(i, c):
        ys = (y + 4 + i) % 8
        block = jnp.concatenate(
            [
                hrows[pl.ds(pl.multiple_of(xs * COL + ys * GRP, GRP), GRP), :]
                for xs in range(4)
            ],
            axis=0,
        )
        out = dot(swap, block).astype(BF)
        for j in range(4):
            rq_send[ys * 4 + j] = out[j * GRP:(j + 1) * GRP]
        for j in range(4):
            qd = ys * 4 + j

            @pl.when(qd != q)
            def _():
                remote(
                    rq_send.at[qd], rq.at[q], rq_s, rq_r.at[(ys - y) % 8], dev_q(qd)
                )

            @pl.when(qd == q)
            def _():
                rq[q] = rq_send[qd]
        return c

    lax.fori_loop(0, 8, return_group, 0)

    wait_for(hq.at[pl.ds(0, 31)], hq_r)

    def order_hidden(g, c):
        block = jnp.concatenate([hq[g * 4 + j] for j in range(4)], axis=0)
        out = dot(swap, block).astype(BF)
        for xs in range(4):
            hrows[pl.ds(pl.multiple_of(xs * COL + g * GRP, GRP), GRP), :] = out[
                xs * GRP:(xs + 1) * GRP
            ]
        return c

    lax.fori_loop(0, 8, order_hidden, 0)
    for c in range(2):
        for half in range(4):
            lanes = (c * 8 + half * 2) * LANE
            wg_vmem[:, lanes:lanes + 256] = dot_tn(
                hrows[...], rows[:, lanes:lanes + 256]
            ).astype(BF)
            for z_ in (half * 2, half * 2 + 1):
                pltpu.make_async_copy(
                    wg_vmem.at[:, pl.ds((c * 8 + z_) * LANE, LANE)],
                    weight_grad.at[0, :, pl.ds(feature_block(c, z_), LANE)],
                    o_sem,
                ).start()

    def relay_back(i, c):
        dy = (4 + i) % 8
        g = (y - dy) % 8

        @pl.when(dy == 0)
        def _():
            wait_for(rq.at[pl.ds(0, 3)], rq_r.at[dy])

        @pl.when(dy != 0)
        def _():
            wait_for(rq.at[pl.ds(0, 4)], rq_r.at[dy])

        block = jnp.concatenate([rq[g * 4 + j] for j in range(4)], axis=0)
        out = dot(swap, block).astype(BF)
        place = pl.ds(pl.multiple_of(g * GRP, GRP), GRP)
        for xs in range(4):
            r2[xs, place, :] = out[xs * GRP:(xs + 1) * GRP]
        rx[x, place, :] = r2[x, place, :]
        for dx in (2, 1, 3):
            xd = (x + dx) % 4
            remote(
                r2.at[xd, place], rx.at[x, place], rx_s, rx_r.at[dx],
                dev(xd, y, z, core),
            )
        return c

    lax.fori_loop(0, 8, relay_back, 0)

    def make_undo(i, c):
        place = pl.ds(pl.multiple_of(i * 128, 128), 128)
        at = lax.broadcasted_iota(jnp.int32, (128, NX * COL), 1)
        undo[place, :] = jnp.where(at == tgt_col[place, :], 1.0, 0.0).astype(BF)
        return c

    lax.fori_loop(0, 8, make_undo, 0)
    for dx in range(1, 4):
        wait_for(rx.at[0], rx_r.at[dx])
    ones = jnp.ones((8, LANE), BF)

    def take(i, c):
        place = pl.ds(pl.multiple_of(i * 256, 256), 256)
        grads = dot(undo[place, :], rx[...].reshape(NX * COL, UNITS))
        slot_grads[place, :] = grads.astype(BF)
        product = hidden[place, :].astype(F32) * grads
        total = product[:, 0:128] + product[:, 128:256] + product[:, 256:384]
        high = total.astype(BF)
        rest = total - high.astype(F32)
        middle = rest.astype(BF)
        low = (rest - middle.astype(F32)).astype(BF)
        gate_recv[hid, :, place] = (
            dot_nt(ones, high) + dot_nt(ones, middle) + dot_nt(ones, low)
        )
        return c

    lax.fori_loop(0, 4, take, 0)

    for d in range(1, 4):
        remote(
            gate_recv.at[hid], gate_recv.at[hid], gt_s, gt_r.at[d],
            (blk, (hid + d) % 4),
        )
    for d in range(1, 4):
        wait_for(gate_recv.at[0], gt_r.at[d])
    gate_out[...] = (gate_recv[0] + gate_recv[1]) + (gate_recv[2] + gate_recv[3])

    wait_for(stage.at[pl.ds(0, 3)], ex_s)
    wait_for(cols.at[0, pl.ds(0, 7)], ra_s)
    wait_for(cols.at[pl.ds(0, 7)], rb_s)
    wait_for(sendx.at[:, pl.ds(1, 7)], x_s)
    wait_for(hs.at[pl.ds(1, 3)], hx_s)
    wait_for(hq_send.at[pl.ds(0, 31)], hq_s)
    wait_for(rq_send.at[pl.ds(0, 31)], rq_s)
    wait_for(r2.at[pl.ds(0, 3)], rx_s)
    wait_for(gate_recv.at[pl.ds(0, 3)], gt_s)
    wait_for(wg_vmem, o_sem)


def fused(og, ids16, weighted, hidden, tgt_row, tgt_col, perm, weight):
    vmem = pl.BlockSpec(memory_space=pltpu.VMEM)
    hbm = pl.BlockSpec(memory_space=pl.ANY)
    dma = pltpu.SemaphoreType.DMA
    buf = lambda *shape: pltpu.VMEM(shape, BF)
    return pl.pallas_call(
        kernel,
        out_shape=(
            jax.ShapeDtypeStruct((SLOTS, UNITS), BF),
            jax.ShapeDtypeStruct((8, SLOTS), F32),
            jax.ShapeDtypeStruct((1, UNITS, FEATS), BF),
        ),
        in_specs=[vmem] * 7 + [hbm],
        out_specs=(vmem, vmem, hbm),
        scratch_shapes=[
            buf(QUAD, TOK + 16, LANE),
            buf(QUAD, TOK + 16, LANE),
            buf(8, 8, CHUNK_ROWS, LANE),
            buf(8, 8 * GRP, CHUNK),
            buf(8, 8, COL, LANE),
            buf(2, NX, 8, COL, LANE),
            buf(NX * COL, FEATS),
            buf(NX, COL, UNITS),
            buf(NX, COL, UNITS),
            buf(NQ, GRP, UNITS),
            buf(NQ, GRP, UNITS),
            buf(NX * COL, UNITS),
            buf(NQ, GRP, UNITS),
            buf(NQ, GRP, UNITS),
            buf(NX, COL, UNITS),
            buf(NX, COL, UNITS),
            buf(SLOTS, NX * COL),
            buf(UNITS, FEATS),
            buf(UNITS, FEATS),
            pltpu.VMEM((4, 8, SLOTS), F32),
            dma, dma((4,)),
            dma, dma((2, 5)),
            dma, dma((2, 5, 2)),
            dma, dma((4,)),
            dma, dma((4,)),
            dma, dma,
            dma, dma((8,)),
            dma, dma((4,)),
            dma, dma((4,)),
            dma, dma,
        ],
        compiler_params=pltpu.CompilerParams(
            collective_id=0, has_side_effects=True, vmem_limit_bytes=60 * 1024 * 1024
        ),
        cost_estimate=pl.CostEstimate(
            flops=20_000_000_000, bytes_accessed=8_000_000, transcendentals=0
        ),
    )(og, ids16, weighted, hidden, tgt_row, tgt_col, perm, weight)


def swap_matrix():
    at = np.arange(4 * GRP)
    outer, inner, row = at // GRP, at % GRP // CAP, at % CAP
    matrix = np.zeros((4 * GRP, 4 * GRP), np.float32)
    matrix[at, inner * GRP + outer * CAP + row] = 1.0
    return matrix


def shards(out_grad, hidden, gates, expert_ids, down_weight):
    onehot = (
        expert_ids[:, :, None] == jnp.arange(128, dtype=jnp.int32)[None, None, :]
    ).astype(F32)
    named = jnp.sum(onehot, axis=1)
    before = jnp.asarray(np.tril(np.ones((TOK, TOK), np.float32), -1), BF)
    count = dot(before, named.astype(BF))
    rank = jnp.sum(onehot * count[:, None, :], axis=2).astype(jnp.int32)
    target = expert_ids * CAP + rank
    weighted = (gates[:, :, None] * hidden.astype(F32)).astype(BF)
    ids16 = jnp.concatenate(
        [expert_ids.T.astype(BF), jnp.zeros((8, TOK), BF)], axis=0
    )
    slot_grads, gate_grad, weight_grad = fused(
        out_grad,
        ids16,
        weighted.reshape(SLOTS, UNITS),
        hidden.reshape(SLOTS, UNITS),
        target.reshape(1, SLOTS),
        target.reshape(SLOTS, 1),
        jnp.asarray(swap_matrix(), BF),
        down_weight,
    )
    slot_grads = slot_grads.reshape(TOK, 8, UNITS).astype(F32)
    hidden_grad = (gates[:, :, None] * slot_grads).astype(BF)
    return weight_grad, hidden_grad, gate_grad[0].reshape(TOK, 8)


def solution(mesh):
    placed = (
        P("blk", "hid"),
        P("blk", None, "hid"),
        P("blk", None),
        P("blk", None),
        P("blk", "hid", None),
    )
    return jax.shard_map(
        shards,
        mesh=mesh,
        in_specs=placed,
        out_specs=(P("blk", "hid", None), P("blk", None, "hid"), P("blk", None)),
        check_vma=False,
    )
```

time: 421 us -> 201 us (0.48); the launches traced: 415 us -> 200 us
  blocking collectives: 263 us -> 0 us
  Pallas kernels: 0 us -> 187 us
  local copies, waits for them, and re-layouts: 51.1 us -> 6.73 us
  waiting for transfers between devices: 44 us -> 0 us
  starting transfers between devices: 22 us -> 0 us
  matrix products: 19.1 us -> 0.89 us
  other arithmetic: 14.3 us -> 4.83 us
    all_to_all x1 -> x0, blocking collectives: 207 us -> none  [shards(): lax.all_to_all(send_grads, 'blk', split_axis=0, concat_axis=0, tiled=True)]
    pallas_call x0 -> x1, Pallas kernels: none -> 187 us  [fused(): pl.pallas_call(kernel, out_shape=(jax.ShapeDtypeStruct((SLOTS, UNITS), BF...]
    all_to_all x2 -> x0, waiting for transfers between devices: 44 us -> none  [the longest x1 40.5 us: shards(): lax.all_to_all(pre_grad.reshape(experts, capacity, unit_count), 'blk', sp...]
    psum x1 -> x0, blocking collectives: 38.7 us -> none  [shards(): gate_grad = lax.psum(partial_value, 'hid')]
    gather x5 -> x0, local copies, waits for them, and re-layouts: 29.5 us -> none  [the longest x2 17.7 us: shards(): full_rows[token_of]]
    all_to_all x2 -> x0, starting transfers between devices: 22 us -> none  [the longest x1 13 us: shards(): lax.all_to_all(pre_grad.reshape(experts, capacity, unit_count), 'blk', sp...]
    dot_general x2 -> x1, matrix products: 19.1 us -> 0.89 us  [dot(): return jnp.dot(a, b, preferred_element_type=F32)]
    all_gather x1 -> x0, blocking collectives: 17.7 us -> none  [shards(): full_rows = lax.all_gather(out_grad, 'hid', axis=1, tiled=True)]
  transfers between devices with their start and end apart: 2 -> 0, of which waited for: 2 -> 0; matrix products, arithmetic and copies ran while one was open for 1% -> 0% of each run, Pallas kernels for 0% -> 0%
where the time goes in v1:
time: 201 us; the launch traced here: 200 us
  Pallas kernels  187 us (93%)
  local copies, waits for them, and re-layouts  6.73 us (3%)
  other arithmetic  4.83 us (2%)
    pallas_call x1, Pallas kernels, fused(): pl.pallas_call(kernel, out_shape=(jax.ShapeDtypeStruct((SLOTS, UNITS), BF...  187 us

profile of v1, /device:TPU:1, one launch (start us, length us, event | category | flops | bytes accessed | tf_op | source)
XLA Modules:
  0.0 200.4 jit_solution(15926211533079179924)
XLA Ops:
  0.6 0.0 copy-start.1
  0.6 0.9 copy.28
  1.5 0.2 convert_reduce_fusion
  1.7 0.9 fusion.4
  2.6 0.4 select_reduce_fusion
  3.1 0.8 convert_add_fusion
  3.9 0.1 copy.30
  4.0 1.0 reshape.29.tgt_col
  4.9 0.7 reshape.26.tgt_row
  5.6 0.6 concatenate.3.ids16
  6.2 0.8 copy.27
  7.0 0.0 copy-done.1
  7.0 1.1 fusion.1.weighted
  8.1 187.3 %shard_map.94 = (bf16[1024,384]{1,0:T(8,128)(2,1)}, f32[8,1024]{1,0:T(8,128)}, bf16[1,384,2048]{2,1,0:T(8,128)(2,1)}) custom-call(bf16[128,512]{1,0:T(8,128)(2,1)} %og.1, bf16[16,128]{1,0:T(8,128)(2,1)} %concatenate.3.ids16, bf16[1024,384]{1,0:T(8,128)(2,1)} %fusion.1.weighted, bf16[1024,384]{1,0:T(8,128)(2,1)} %bitcast.10, s32[1,1024]{1,0:T(1,128)} %reshape.26.tgt_row, ...), custom_call_target="tpu_custom_call" | custom-call | flops 20000000000 | bytes 8000000 | tf_op jit(solution)/shard_map/pallas_call | solution.py:442
  195.4 0.0 copy-start
  195.4 2.3 %fusion = bf16[128,8,384]{2,1,0:T(8,128)(2,1)} fusion(bf16[1024,384]{1,0:T(8,128)(2,1)} %get-tuple-element.7, f32[128,8]{1,0:T(8,128)S(1)} %copy.27), kind=kLoop, calls=%fused_computation.1 | loop fusion | flops 1179648 | bytes 1576960 | tf_op jit(solution)/shard_map/convert_element_type | solution.py:524
  197.8 0.8 slice_reduce_fusion
  198.5 0.1 reshape_squeeze.3
  198.6 0.7 copy.33
  199.3 0.0 copy-done
  199.3 1.1 copy.35
  (1 shorter events, 0.0 us)
Async XLA Ops:
  0.6 6.4 %copy-start.1 = (bf16[128,8,384]{2,1,0:T(8,128)(2,1)S(1)}, bf16[128,8,384]{2,1,0:T(8,128)(2,1)}, u32[]{:S(2)}) copy-start(bf16[128,8,384]{2,1,0:T(8,128)(2,1)} %param.8) | copy-start | bytes 2359300
  195.4 3.9 %copy-start = (bf16[1,384,2048]{2,1,0:T(8,128)(2,1)S(1)}, bf16[1,384,2048]{2,1,0:T(8,128)(2,1)}, u32[]{:S(2)}) copy-start(bf16[1,384,2048]{2,1,0:T(8,128)(2,1)} %get-tuple-element.26) | copy-start | bytes 4718596

commit v2 on v1

--- a/solution.py
+++ b/solution.py
@@ -1,8 +1,5 @@
-import functools
-
 import jax
 import jax.numpy as jnp
-import numpy as np
 from jax import lax
 from jax.experimental import pallas as pl
 from jax.experimental.pallas import tpu as pltpu
@@ -38,12 +35,19 @@
     return lax.dot_general(a, b, (((0,), (0,)), ((), ())), preferred_element_type=F32)
 
 
+def thirds(value):
+    high = value.astype(BF)
+    rest = value - high.astype(F32)
+    middle = rest.astype(BF)
+    return high, middle, (rest - middle.astype(F32)).astype(BF)
+
+
 def kernel(
-    og, ids16, weighted, hidden, tgt_row, tgt_col, perm, weight,
-    slot_grads, gate_out, weight_grad,
-    stage, ex, cols, gsel, sendx, recvx, rows,
+    og, hidden, gates, ids, weight,
+    hidden_grad, gate_out, weight_grad,
+    weighted, slot_target, slot_gate, stage, ex, cols, gsel, sendx, recvx, rows,
     hs, hx, hq_send, hq, hrows,
-    rq_send, rq, r2, rx, undo, w_vmem, wg_vmem, gate_recv,
+    rq_send, rq, r2, rx, undo, w_vmem, wg_vmem, gate_row, gate_recv,
     ex_s, ex_r, ra_s, ra_r, rb_s, rb_r, x_s, x_r,
     hx_s, hx_r, hq_s, hq_r, rq_s, rq_r, rx_s, rx_r, gt_s, gt_r, w_sem, o_sem,
 ):
@@ -114,10 +118,81 @@
                 w_sem,
             ).start()
 
+    lane = lax.broadcasted_iota(jnp.int32, (TOK, LANE), 1)
+    own_ids = ids[...].astype(F32)
+    both = jnp.concatenate(
+        [own_ids, gates[...], jnp.zeros((TOK - 16, LANE), F32)], axis=0
+    ).T
+    id_lanes = jnp.where(lane < 8, both, 0.0)
+    gate_lanes = jnp.zeros((TOK, LANE), F32)
+    named = jnp.zeros((TOK, LANE), F32)
+    for k in range(8):
+        gate_lanes = jnp.where(lane % 8 == k, both[:, 8 + k:9 + k], gate_lanes)
+        named = named + jnp.where(lane.astype(F32) == both[:, k:k + 1], 1.0, 0.0)
+    ids16 = jnp.concatenate([own_ids, jnp.zeros((8, TOK), F32)], axis=0).astype(BF)
     for j in range(QUAD):
         stage[j, 0:TOK, :] = og[:, j * LANE:(j + 1) * LANE]
-        stage[j, TOK:TOK + 16, :] = ids16[...]
-
+        stage[j, TOK:TOK + 16, :] = ids16
+
+    high, middle, low = (part.astype(F32) for part in thirds(gate_lanes))
+    mixed = jnp.where(
+        lane < 8, high,
+        jnp.where(lane < 16, middle, jnp.where(lane < 24, low, 0.0)),
+    )
+    earlier = jnp.where(
+        lax.broadcasted_iota(jnp.int32, (TOK, TOK), 1)
+        < lax.broadcasted_iota(jnp.int32, (TOK, TOK), 0), 1.0, 0.0,
+    ).astype(BF)
+    count = dot(earlier, named.astype(BF)).astype(BF)
+    slot = lax.broadcasted_iota(jnp.int32, (SLOTS, LANE), 0)
+    slot_lane = lax.broadcasted_iota(jnp.int32, (SLOTS, LANE), 1)
+    token_of = jnp.where(slot // 8 == slot_lane, 1.0, 0.0).astype(BF)
+    turn = slot % 8 == slot_lane % 8
+    slot_gate[...] = jnp.broadcast_to(
+        jnp.sum(
+            jnp.where(turn, dot(token_of, mixed.astype(BF)), 0.0), axis=1, keepdims=True
+        ),
+        (SLOTS, LANE),
+    )
+    slot_id = jnp.sum(
+        jnp.where(turn, dot(token_of, id_lanes.astype(BF)), 0.0), axis=1, keepdims=True
+    )
+    slot_rank = jnp.sum(
+        jnp.where(slot_lane.astype(F32) == slot_id, dot(token_of, count), 0.0),
+        axis=1, keepdims=True,
+    )
+    slot_target[...] = jnp.broadcast_to(slot_id * float(CAP) + slot_rank, (SLOTS, LANE))
+    both = jnp.where(
+        slot_lane == 0, slot_id, jnp.where(slot_lane == 1, slot_rank, 0.0)
+    ).astype(BF)
+    lane16 = lax.broadcasted_iota(jnp.int32, (16, LANE), 1)
+    tgt_row = dot_nt(
+        jnp.where(lane16 == 0, float(CAP), jnp.where(lane16 == 1, 1.0, 0.0)).astype(BF),
+        both,
+    )[0:1]
+    for i in range(4):
+        part = slice(i * 256, (i + 1) * 256)
+        for j in range(3):
+            weighted[part, j * LANE:(j + 1) * LANE] = (
+                slot_gate[part, :] * hidden[part, j * LANE:(j + 1) * LANE].astype(F32)
+            ).astype(BF)
+
+    def select_hidden(dx):
+        xd = (x + dx) % 4
+        at = lax.broadcasted_iota(jnp.int32, (COL, SLOTS), 0) + xd * COL
+        pick = jnp.where(at.astype(F32) == tgt_row, 1.0, 0.0).astype(BF)
+        picked = dot(pick, weighted[...]).astype(BF)
+        if dx == 0:
+            hx[x] = picked
+        else:
+            hs[dx] = picked
+
+    def send_hidden_x(dx):
+        remote(
+            hs.at[dx], hx.at[x], hx_s, hx_r.at[dx], dev((x + dx) % 4, y, z, core)
+        )
+
+    select_hidden(2)
     pl.semaphore_wait(barrier, greeted)
 
     for d in range(1, 4):
@@ -128,22 +203,9 @@
         )
     ex[quad] = stage[quad]
 
-    def select_hidden(dx):
-        xd = (x + dx) % 4
-        at = lax.broadcasted_iota(jnp.int32, (COL, SLOTS), 0) + xd * COL
-        pick = jnp.where(at == tgt_row[...], 1.0, 0.0).astype(BF)
-        picked = dot(pick, weighted[...]).astype(BF)
-        if dx == 0:
-            hx[x] = picked
-        else:
-            hs[dx] = picked
-            remote(
-                hs.at[dx], hx.at[x], hx_s, hx_r.at[dx],
-                dev(xd, y, z, core),
-            )
-
-    for dx in (2, 1, 3, 0):
-        select_hidden(dx)
+    send_hidden_x(2)
+    select_hidden(1)
+    send_hidden_x(1)
 
     for d in range(1, 4):
         wait_for(ex.at[0], ex_r.at[d])
@@ -164,23 +226,31 @@
             if step == 4:
                 ref = cols.at[pb, a, pl.ds(way * half_rows, half_rows)]
             remote(ref, ref, ra_s, ra_r.at[way, step], dev_ab((pa + sign) % 8, pb))
+        if step == 1:
+            select_hidden(3)
+            send_hidden_x(3)
+        if step == 2:
+            select_hidden(0)
     for way in range(2):
         wait_for(cols.at[0, 0, pl.ds(0, half_rows)], ra_r.at[way, 4])
 
+    def ring_has(step, way, piece):
+        return step < 4 or piece // 2 == way
+
     def ring_wait(step):
-        for way in range(2):
-            for piece in range(2):
-                if step < 4 or piece == way:
-                    wait_for(cols.at[0, pl.ds(0, 4)], rb_r.at[way, step, piece])
+        for piece in range(4):
+            for way in range(2):
+                if ring_has(step, way, piece):
+                    wait_for(cols.at[0, pl.ds(0, 2)], rb_r.at[way, step, piece])
 
     def ring_send(step):
-        for way, sign in ((0, 1), (1, -1)):
-            b = (pb - sign * (step - 1)) % 8
-            for piece in range(2):
+        for piece in range(4):
+            for way, sign in ((0, 1), (1, -1)):
+                b = (pb - sign * (step - 1)) % 8
                 if step > 1:
-                    wait_for(cols.at[0, pl.ds(0, 4)], rb_r.at[way, step - 1, piece])
-                if step < 4 or piece == way:
-                    ref = cols.at[b, pl.ds(4 * piece, 4)]
+                    wait_for(cols.at[0, pl.ds(0, 2)], rb_r.at[way, step - 1, piece])
+                if ring_has(step, way, piece):
+                    ref = cols.at[b, pl.ds(2 * piece, 2)]
                     remote(
                         ref, ref, rb_s, rb_r.at[way, step, piece],
                         dev_ab(pa, (pb + sign) % 8),
@@ -254,9 +324,22 @@
     select((pb - 1) % 8, False)
     select((pb + 1) % 8, False)
 
+    ring_send(3)
+    select((pb - 2) % 8, False)
+    select((pb + 2) % 8, False)
+    ring_send(4)
+    select((pb - 3) % 8, False)
+    select((pb + 3) % 8, False)
+
     for dx in range(1, 4):
         wait_for(hx.at[0], hx_r.at[dx])
-    swap = perm[...]
+    out_row = lax.broadcasted_iota(jnp.int32, (4 * GRP, 4 * GRP), 0)
+    outer = sum(jnp.where(out_row >= n * GRP, 1, 0) for n in range(1, 4))
+    within = out_row - outer * GRP
+    inner = sum(jnp.where(within >= n * CAP, 1, 0) for n in range(1, 4))
+    from_row = inner * GRP + outer * CAP + within - inner * CAP
+    in_row = lax.broadcasted_iota(jnp.int32, (4 * GRP, 4 * GRP), 1)
+    swap = jnp.where(in_row == from_row, 1.0, 0.0).astype(BF)
 
     def relay_hidden(g, c):
         block = jnp.concatenate(
@@ -278,12 +361,6 @@
 
     lax.fori_loop(1, 32, send_hidden, 0)
 
-    ring_send(3)
-    select((pb - 2) % 8, False)
-    select((pb + 2) % 8, False)
-    ring_send(4)
-    select((pb - 3) % 8, False)
-    select((pb + 3) % 8, False)
     ring_wait(4)
     select((pb + 4) % 8, False)
 
@@ -387,8 +464,11 @@
 
     def make_undo(i, c):
         place = pl.ds(pl.multiple_of(i * 128, 128), 128)
-        at = lax.broadcasted_iota(jnp.int32, (128, NX * COL), 1)
-        undo[place, :] = jnp.where(at == tgt_col[place, :], 1.0, 0.0).astype(BF)
+        for j in range(NX * COL // LANE):
+            at = lax.broadcasted_iota(jnp.int32, (128, LANE), 1) + j * LANE
+            undo[place, j * LANE:(j + 1) * LANE] = jnp.where(
+                at.astype(F32) == slot_target[place, :], 1.0, 0.0
+            ).astype(BF)
         return c
 
     lax.fori_loop(0, 8, make_undo, 0)
@@ -399,19 +479,23 @@
     def take(i, c):
         place = pl.ds(pl.multiple_of(i * 256, 256), 256)
         grads = dot(undo[place, :], rx[...].reshape(NX * COL, UNITS))
-        slot_grads[place, :] = grads.astype(BF)
+        for j in range(3):
+            part = slice(j * LANE, (j + 1) * LANE)
+            hidden_grad[place, part] = (slot_gate[place, :] * grads[:, part]).astype(BF)
         product = hidden[place, :].astype(F32) * grads
         total = product[:, 0:128] + product[:, 128:256] + product[:, 256:384]
-        high = total.astype(BF)
-        rest = total - high.astype(F32)
-        middle = rest.astype(BF)
-        low = (rest - middle.astype(F32)).astype(BF)
-        gate_recv[hid, :, place] = (
-            dot_nt(ones, high) + dot_nt(ones, middle) + dot_nt(ones, low)
-        )
+        gate_row[:, place] = sum(dot_nt(ones, part) for part in thirds(total))
         return c
 
     lax.fori_loop(0, 4, take, 0)
+    in_turn = (
+        lax.broadcasted_iota(jnp.int32, (8, SLOTS), 1) % 8
+        == lax.broadcasted_iota(jnp.int32, (8, SLOTS), 0)
+    )
+    token_of = jnp.where(slot // 8 == slot_lane, 1.0, 0.0).astype(BF)
+    gate_recv[hid] = sum(
+        dot(part, token_of) for part in thirds(jnp.where(in_turn, gate_row[...], 0.0))
+    )
 
     for d in range(1, 4):
         remote(
@@ -434,7 +518,7 @@
     wait_for(wg_vmem, o_sem)
 
 
-def fused(og, ids16, weighted, hidden, tgt_row, tgt_col, perm, weight):
+def fused(og, hidden, gates, ids, weight):
     vmem = pl.BlockSpec(memory_space=pltpu.VMEM)
     hbm = pl.BlockSpec(memory_space=pl.ANY)
     dma = pltpu.SemaphoreType.DMA
@@ -443,12 +527,15 @@
         kernel,
         out_shape=(
             jax.ShapeDtypeStruct((SLOTS, UNITS), BF),
-            jax.ShapeDtypeStruct((8, SLOTS), F32),
+            jax.ShapeDtypeStruct((8, TOK), F32),
             jax.ShapeDtypeStruct((1, UNITS, FEATS), BF),
         ),
-        in_specs=[vmem] * 7 + [hbm],
+        in_specs=[vmem] * 4 + [hbm],
         out_specs=(vmem, vmem, hbm),
         scratch_shapes=[
+            buf(SLOTS, UNITS),
+            pltpu.VMEM((SLOTS, LANE), F32),
+            pltpu.VMEM((SLOTS, LANE), F32),
             buf(QUAD, TOK + 16, LANE),
             buf(QUAD, TOK + 16, LANE),
             buf(8, 8, CHUNK_ROWS, LANE),
@@ -468,10 +555,11 @@
             buf(SLOTS, NX * COL),
             buf(UNITS, FEATS),
             buf(UNITS, FEATS),
-            pltpu.VMEM((4, 8, SLOTS), F32),
+            pltpu.VMEM((8, SLOTS), F32),
+            pltpu.VMEM((4, 8, TOK), F32),
             dma, dma((4,)),
             dma, dma((2, 5)),
-            dma, dma((2, 5, 2)),
+            dma, dma((2, 5, 4)),
             dma, dma((4,)),
             dma, dma((4,)),
             dma, dma,
@@ -486,43 +574,18 @@
         cost_estimate=pl.CostEstimate(
             flops=20_000_000_000, bytes_accessed=8_000_000, transcendentals=0
         ),
-    )(og, ids16, weighted, hidden, tgt_row, tgt_col, perm, weight)
-
-
-def swap_matrix():
-    at = np.arange(4 * GRP)
-    outer, inner, row = at // GRP, at % GRP // CAP, at % CAP
-    matrix = np.zeros((4 * GRP, 4 * GRP), np.float32)
-    matrix[at, inner * GRP + outer * CAP + row] = 1.0
-    return matrix
+    )(og, hidden, gates, ids, weight)
 
 
 def shards(out_grad, hidden, gates, expert_ids, down_weight):
-    onehot = (
-        expert_ids[:, :, None] == jnp.arange(128, dtype=jnp.int32)[None, None, :]
-    ).astype(F32)
-    named = jnp.sum(onehot, axis=1)
-    before = jnp.asarray(np.tril(np.ones((TOK, TOK), np.float32), -1), BF)
-    count = dot(before, named.astype(BF))
-    rank = jnp.sum(onehot * count[:, None, :], axis=2).astype(jnp.int32)
-    target = expert_ids * CAP + rank
-    weighted = (gates[:, :, None] * hidden.astype(F32)).astype(BF)
-    ids16 = jnp.concatenate(
-        [expert_ids.T.astype(BF), jnp.zeros((8, TOK), BF)], axis=0
-    )
-    slot_grads, gate_grad, weight_grad = fused(
+    hidden_grad, gate_grad, weight_grad = fused(
         out_grad,
-        ids16,
-        weighted.reshape(SLOTS, UNITS),
         hidden.reshape(SLOTS, UNITS),
-        target.reshape(1, SLOTS),
-        target.reshape(SLOTS, 1),
-        jnp.asarray(swap_matrix(), BF),
+        gates.T,
+        expert_ids.T,
         down_weight,
     )
-    slot_grads = slot_grads.reshape(TOK, 8, UNITS).astype(F32)
-    hidden_grad = (gates[:, :, None] * slot_grads).astype(BF)
-    return weight_grad, hidden_grad, gate_grad[0].reshape(TOK, 8)
+    return weight_grad, hidden_grad.reshape(TOK, 8, UNITS), gate_grad.T
 
 
 def solution(mesh):

time: 201 us -> 174 us (0.87)
  Pallas kernels: 187 us -> 168 us
  other arithmetic: 4.83 us -> 0 us
  local copies, waits for them, and re-layouts: 6.73 us -> 4.28 us
    pallas_call x1, Pallas kernels: 187 us -> 168 us  [fused(): pl.pallas_call(kernel, out_shape=(jax.ShapeDtypeStruct((SLOTS, UNITS), BF...]
    convert_element_type x1 -> x0, other arithmetic: 2.34 us -> none  [shards(): hidden_grad = (gates[:, :, None] * slot_grads).astype(BF)]
    unnamed x8 -> x7, local copies, waits for them, and re-layouts: 3.46 us -> 4.28 us
where the time goes in v2:
time: 174 us; the launch traced here: 173 us
  Pallas kernels  168 us (97%)
  local copies, waits for them, and re-layouts  4.28 us (2%)
    pallas_call x1, Pallas kernels, fused(): pl.pallas_call(kernel, out_shape=(jax.ShapeDtypeStruct((SLOTS, UNITS), BF...  168 us
    unnamed x7, local copies, waits for them, and re-layouts  4.28 us

profile of v2, /device:TPU:1, one launch (start us, length us, event | category | flops | bytes accessed | tf_op | source)
XLA Modules:
  0.0 173.2 jit_solution(7018553893914714077)
XLA Ops:
  0.6 168.2 %shard_map.76 = (bf16[1024,384]{1,0:T(8,128)(2,1)}, f32[8,128]{1,0:T(8,128)}, bf16[1,384,2048]{2,1,0:T(8,128)(2,1)}) custom-call(bf16[128,512]{1,0:T(8,128)(2,1)} %og.1, bf16[1024,384]{1,0:T(8,128)(2,1)} %bitcast.7, f32[8,128]{1,0:T(8,128)} %bitcast.8, s32[8,128]{1,0:T(8,128)} %bitcast.9, bf16[1,384,2048]{2,1,0:T(8,128)(2,1)} %weight.1), custom_call_target="tpu_custom_call" | custom-call | flops 20000000000 | bytes 8000000 | tf_op jit(solution)/shard_map/pallas_call | solution.py:526
  168.9 0.0 copy-start
  168.9 2.8 %copy.11 = bf16[1,384,2048]{2,1,0:T(8,128)(2,1)} copy(bf16[1,384,2048]{2,1,0:T(8,128)(2,1)} %get-tuple-element.12) | data formatting | bytes 3145728
  171.7 0.0 copy-done
  171.7 0.0 copy-start.1
  171.7 0.9 copy.12
  172.6 0.0 copy-done.1
  172.6 0.6 copy.13
Async XLA Ops:
  168.9 2.8 %copy-start = (bf16[1024,384]{1,0:T(8,128)(2,1)S(1)}, bf16[1024,384]{1,0:T(8,128)(2,1)}, u32[]{:S(2)}) copy-start(bf16[1024,384]{1,0:T(8,128)(2,1)} %get-tuple-element.7) | copy-start | bytes 2359300
  171.7 0.9 copy-start.1

commit v3 on v2

--- a/solution.py
+++ b/solution.py
@@ -45,7 +45,7 @@
 def kernel(
     og, hidden, gates, ids, weight,
     hidden_grad, gate_out, weight_grad,
-    weighted, slot_target, slot_gate, stage, ex, cols, gsel, sendx, recvx, rows,
+    weighted, slot_target, slot_gate, stage, ex, cols, gsel, sendx, rows,
     hs, hx, hq_send, hq, hrows,
     rq_send, rq, r2, rx, undo, w_vmem, wg_vmem, gate_row, gate_recv,
     ex_s, ex_r, ra_s, ra_r, rb_s, rb_r, x_s, x_r,
@@ -84,28 +84,14 @@
         return dev(x, core * a + (1 - core) * b, core * b + (1 - core) * a, core)
 
     barrier = pltpu.get_barrier_semaphore()
-
-    def greet(device):
-        pl.semaphore_signal(barrier, inc=1, device_id=device, device_id_type=MESH)
-
-    greeted = 0
-    for step in (1, 7):
-        greet(dev_ab((pa + step) % 8, pb))
-        greet(dev_ab(pa, (pb + step) % 8))
-        greeted += 2
-    for d in range(1, 8):
-        greet(dev((x + d // 2) % 4, y, z, (core + d % 2) % 2))
-        greeted += 1
-    for d in range(1, 4):
-        greet((blk, (hid + d) % 4))
-        greeted += 1
-
-    def greet_q(d, c):
-        greet(dev_q((q + d) % 32))
-        return c
-
-    lax.fori_loop(1, 32, greet_q, 0)
-    greeted += 31
+    friends = [dev_ab((pa + step) % 8, pb) for step in (1, 7)]
+    friends += [dev_ab(pa, (pb + step) % 8) for step in (1, 7)]
+    friends += [
+        dev((x + d // 2) % 4, y, z, (core + d % 2) % 2) for d in range(1, 8)
+    ]
+    friends += [dev(x, y, (z + 4) % 8, c) for c in range(2)]
+    for friend in friends:
+        pl.semaphore_signal(barrier, inc=1, device_id=friend, device_id_type=MESH)
 
     def feature_block(c, z_):
         return (z_ % 4) * 512 + (z_ // 4) * 256 + c * 128
@@ -170,13 +156,6 @@
         jnp.where(lane16 == 0, float(CAP), jnp.where(lane16 == 1, 1.0, 0.0)).astype(BF),
         both,
     )[0:1]
-    for i in range(4):
-        part = slice(i * 256, (i + 1) * 256)
-        for j in range(3):
-            weighted[part, j * LANE:(j + 1) * LANE] = (
-                slot_gate[part, :] * hidden[part, j * LANE:(j + 1) * LANE].astype(F32)
-            ).astype(BF)
-
     def select_hidden(dx):
         xd = (x + dx) % 4
         at = lax.broadcasted_iota(jnp.int32, (COL, SLOTS), 0) + xd * COL
@@ -192,8 +171,7 @@
             hs.at[dx], hx.at[x], hx_s, hx_r.at[dx], dev((x + dx) % 4, y, z, core)
         )
 
-    select_hidden(2)
-    pl.semaphore_wait(barrier, greeted)
+    pl.semaphore_wait(barrier, len(friends))
 
     for d in range(1, 4):
         other = (quad + d) % 4
@@ -203,9 +181,14 @@
         )
     ex[quad] = stage[quad]
 
+    for i in range(4):
+        part = slice(i * 256, (i + 1) * 256)
+        for j in range(3):
+            weighted[part, j * LANE:(j + 1) * LANE] = (
+                slot_gate[part, :] * hidden[part, j * LANE:(j + 1) * LANE].astype(F32)
+            ).astype(BF)
+    select_hidden(2)
     send_hidden_x(2)
-    select_hidden(1)
-    send_hidden_x(1)
 
     for d in range(1, 4):
         wait_for(ex.at[0], ex_r.at[d])
@@ -227,9 +210,12 @@
                 ref = cols.at[pb, a, pl.ds(way * half_rows, half_rows)]
             remote(ref, ref, ra_s, ra_r.at[way, step], dev_ab((pa + sign) % 8, pb))
         if step == 1:
+            select_hidden(1)
+            send_hidden_x(1)
+        if step == 2:
             select_hidden(3)
             send_hidden_x(3)
-        if step == 2:
+        if step == 3:
             select_hidden(0)
     for way in range(2):
         wait_for(cols.at[0, 0, pl.ds(0, half_rows)], ra_r.at[way, 4])
@@ -241,16 +227,28 @@
         for piece in range(4):
             for way in range(2):
                 if ring_has(step, way, piece):
-                    wait_for(cols.at[0, pl.ds(0, 2)], rb_r.at[way, step, piece])
+                    wait_for(cols.at[0, pl.ds(0, 2), pl.ds(0, CHUNK)], rb_r.at[way, step, piece])
+        wait_for(cols.at[0, 0, pl.ds(CHUNK, 32)], rb_r.at[0, step, 4])
 
     def ring_send(step):
+        for way, sign in ((0, 1), (1, -1)):
+            if step > 1:
+                wait_for(cols.at[0, 0, pl.ds(CHUNK, 32)], rb_r.at[way, step - 1, 4])
+            if step < 4 or way == 0:
+                ref = cols.at[(pb - sign * (step - 1)) % 8, 0, pl.ds(CHUNK, 32)]
+                remote(
+                    ref, ref, rb_s, rb_r.at[way, step, 4], dev_ab(pa, (pb + sign) % 8)
+                )
         for piece in range(4):
             for way, sign in ((0, 1), (1, -1)):
                 b = (pb - sign * (step - 1)) % 8
                 if step > 1:
-                    wait_for(cols.at[0, pl.ds(0, 2)], rb_r.at[way, step - 1, piece])
+                    wait_for(
+                        cols.at[0, pl.ds(0, 2), pl.ds(0, CHUNK)],
+                        rb_r.at[way, step - 1, piece],
+                    )
                 if ring_has(step, way, piece):
-                    ref = cols.at[b, pl.ds(2 * piece, 2)]
+                    ref = cols.at[b, pl.ds(2 * piece, 2), pl.ds(0, CHUNK)]
                     remote(
                         ref, ref, rb_s, rb_r.at[way, step, piece],
                         dev_ab(pa, (pb + sign) % 8),
@@ -304,42 +302,34 @@
 
         def one_chunk(a, c):
             col = core * a + (1 - core) * b
+            block = core * b + (1 - core) * a
             out = dot(gsel[col], cols[b, a, 0:CHUNK, :]).astype(BF)
-            place = pl.ds(pl.multiple_of(a * GRP, GRP), GRP)
-            recvx[core, x, b, place, :] = out[0:GRP]
+            lanes = pl.multiple_of(block * LANE, LANE)
+            rows[
+                pl.ds(pl.multiple_of((col * 4 + x) * GRP, GRP), GRP),
+                pl.ds(pl.multiple_of(core * (FEATS // 2) + lanes, LANE), LANE),
+            ] = out[0:GRP]
             for e in range(1, 8):
-                sendx[b, e, place, :] = out[e * GRP:(e + 1) * GRP]
+                sendx[col, e, :, pl.ds(lanes, LANE)] = out[e * GRP:(e + 1) * GRP]
             return c
 
         lax.fori_loop(0, 8, one_chunk, 0)
+
+        @pl.when(core == 0)
+        def _():
+            send_column(b)
+
+    def send_column(col):
+        place = pl.ds(pl.multiple_of((col * 4 + x) * GRP, GRP), GRP)
+        half = pl.ds(pl.multiple_of(core * (FEATS // 2), FEATS // 2), FEATS // 2)
         for e in (4, 5, 2, 3, 6, 7, 1):
             remote(
-                sendx.at[b, e], recvx.at[core, x, b], x_s, x_r.at[e // 2],
+                sendx.at[col, e], rows.at[place, half], x_s, x_r.at[(col - y) % 8],
                 dev((x + e // 2) % 4, y, z, (core + e % 2) % 2),
             )
 
-    ring_send(1)
-    select(pb, True)
-    ring_send(2)
-    select((pb - 1) % 8, False)
-    select((pb + 1) % 8, False)
-
-    ring_send(3)
-    select((pb - 2) % 8, False)
-    select((pb + 2) % 8, False)
-    ring_send(4)
-    select((pb - 3) % 8, False)
-    select((pb + 3) % 8, False)
-
-    for dx in range(1, 4):
-        wait_for(hx.at[0], hx_r.at[dx])
-    out_row = lax.broadcasted_iota(jnp.int32, (4 * GRP, 4 * GRP), 0)
-    outer = sum(jnp.where(out_row >= n * GRP, 1, 0) for n in range(1, 4))
-    within = out_row - outer * GRP
-    inner = sum(jnp.where(within >= n * CAP, 1, 0) for n in range(1, 4))
-    from_row = inner * GRP + outer * CAP + within - inner * CAP
-    in_row = lax.broadcasted_iota(jnp.int32, (4 * GRP, 4 * GRP), 1)
-    swap = jnp.where(in_row == from_row, 1.0, 0.0).astype(BF)
+    def outward(i):
+        return (1 - 2 * (i % 2)) * ((i + 1) // 2)
 
     def relay_hidden(g, c):
         block = jnp.concatenate(
@@ -351,46 +341,66 @@
             hq_send[g * 4 + j] = out[j * GRP:(j + 1) * GRP]
         return c
 
-    lax.fori_loop(0, 8, relay_hidden, 0)
-    hq[q] = hq_send[q]
-
     def send_hidden(d, c):
         qd = (q + d) % 32
         remote(hq_send.at[qd], hq.at[q], hq_s, hq_r, dev_q(qd))
         return c
 
-    lax.fori_loop(1, 32, send_hidden, 0)
-
+    def make_undo(i, c):
+        place = pl.ds(pl.multiple_of(i * 128, 128), 128)
+        for j in range(NX * COL // LANE):
+            at = lax.broadcasted_iota(jnp.int32, (128, LANE), 1) + j * LANE
+            undo[place, j * LANE:(j + 1) * LANE] = jnp.where(
+                at.astype(F32) == slot_target[place, :], 1.0, 0.0
+            ).astype(BF)
+        return c
+
+    out_row = lax.broadcasted_iota(jnp.int32, (4 * GRP, 4 * GRP), 0)
+    outer = sum(jnp.where(out_row >= n * GRP, 1, 0) for n in range(1, 4))
+    within = out_row - outer * GRP
+    inner = sum(jnp.where(within >= n * CAP, 1, 0) for n in range(1, 4))
+    from_row = inner * GRP + outer * CAP + within - inner * CAP
+    in_row = lax.broadcasted_iota(jnp.int32, (4 * GRP, 4 * GRP), 1)
+    swap = jnp.where(in_row == from_row, 1.0, 0.0).astype(BF)
+
+    ring_send(1)
+    select(pb, True)
+    ring_send(2)
+    select((pb - 1) % 8, False)
+    select((pb + 1) % 8, False)
+    ring_send(3)
+    select((pb - 2) % 8, False)
+    select((pb + 2) % 8, False)
+    for dx in range(1, 4):
+        wait_for(hx.at[0], hx_r.at[dx])
+    lax.fori_loop(0, 8, relay_hidden, 0)
+    hq[q] = hq_send[q]
+    ring_send(4)
+    select((pb - 3) % 8, False)
+    select((pb + 3) % 8, False)
     ring_wait(4)
     select((pb + 4) % 8, False)
 
+    @pl.when(core == 1)
+    def _():
+        send_column(y)
+        send_column((y + outward(1)) % 8)
+
+    lax.fori_loop(1, 32, send_hidden, 0)
+    lax.fori_loop(0, 8, make_undo, 0)
     wait_for(w_vmem, w_sem)
-    for dx in (0, 1, 3, 2):
-        xs = (x - dx) % 4
-        if dx == 0:
-            wait_for(recvx.at[0, 0], x_r.at[0])
-        else:
-            wait_for(recvx.at[:, 0], x_r.at[dx])
-        place = pl.ds(pl.multiple_of(xs * COL, COL), COL)
-        for a in range(8):
-            rows[place, a * LANE:(a + 1) * LANE] = recvx[
-                0, xs, :, a * GRP:(a + 1) * GRP, :
-            ].reshape(COL, LANE)
-            rows[place, FEATS // 2 + a * LANE:FEATS // 2 + (a + 1) * LANE] = recvx[
-                1, xs, a
-            ]
-        hrows[place, :] = dot_nt(rows[place, :], w_vmem[...]).astype(BF)
-
-    def return_group(i, c):
-        ys = (y + 4 + i) % 8
-        block = jnp.concatenate(
-            [
-                hrows[pl.ds(pl.multiple_of(xs * COL + ys * GRP, GRP), GRP), :]
-                for xs in range(4)
-            ],
-            axis=0,
-        )
-        out = dot(swap, block).astype(BF)
+
+    def one_column(i):
+        ys = (y + outward(i)) % 8
+        wait_for(sendx.at[0, pl.ds(1, 7)], x_r.at[outward(i) % 8])
+
+        @pl.when((core == 1) & (i < 6))
+        def _():
+            send_column((y + outward(i + 2)) % 8)
+
+        block = rows[pl.ds(pl.multiple_of(ys * 4 * GRP, GRP), 4 * GRP), :]
+        pre = dot_nt(block, w_vmem[...]).astype(BF)
+        out = dot(swap, pre).astype(BF)
         for j in range(4):
             rq_send[ys * 4 + j] = out[j * GRP:(j + 1) * GRP]
         for j in range(4):
@@ -405,38 +415,10 @@
             @pl.when(qd == q)
             def _():
                 rq[q] = rq_send[qd]
-        return c
-
-    lax.fori_loop(0, 8, return_group, 0)
-
-    wait_for(hq.at[pl.ds(0, 31)], hq_r)
-
-    def order_hidden(g, c):
-        block = jnp.concatenate([hq[g * 4 + j] for j in range(4)], axis=0)
-        out = dot(swap, block).astype(BF)
-        for xs in range(4):
-            hrows[pl.ds(pl.multiple_of(xs * COL + g * GRP, GRP), GRP), :] = out[
-                xs * GRP:(xs + 1) * GRP
-            ]
-        return c
-
-    lax.fori_loop(0, 8, order_hidden, 0)
-    for c in range(2):
-        for half in range(4):
-            lanes = (c * 8 + half * 2) * LANE
-            wg_vmem[:, lanes:lanes + 256] = dot_tn(
-                hrows[...], rows[:, lanes:lanes + 256]
-            ).astype(BF)
-            for z_ in (half * 2, half * 2 + 1):
-                pltpu.make_async_copy(
-                    wg_vmem.at[:, pl.ds((c * 8 + z_) * LANE, LANE)],
-                    weight_grad.at[0, :, pl.ds(feature_block(c, z_), LANE)],
-                    o_sem,
-                ).start()
-
-    def relay_back(i, c):
-        dy = (4 + i) % 8
-        g = (y - dy) % 8
+
+    def relay_back(i):
+        dy = outward(i) % 8
+        g = (y - outward(i)) % 8
 
         @pl.when(dy == 0)
         def _():
@@ -458,20 +440,44 @@
                 r2.at[xd, place], rx.at[x, place], rx_s, rx_r.at[dx],
                 dev(xd, y, z, core),
             )
+
+    def column_and_relay(i, c):
+        one_column(i)
+
+        @pl.when(i >= 2)
+        def _():
+            relay_back(i - 2)
+
         return c
 
-    lax.fori_loop(0, 8, relay_back, 0)
-
-    def make_undo(i, c):
-        place = pl.ds(pl.multiple_of(i * 128, 128), 128)
-        for j in range(NX * COL // LANE):
-            at = lax.broadcasted_iota(jnp.int32, (128, LANE), 1) + j * LANE
-            undo[place, j * LANE:(j + 1) * LANE] = jnp.where(
-                at.astype(F32) == slot_target[place, :], 1.0, 0.0
+    lax.fori_loop(0, 8, column_and_relay, 0)
+
+    def order_hidden(g, c):
+        block = jnp.concatenate([hq[g * 4 + j] for j in range(4)], axis=0)
+        hrows[pl.ds(pl.multiple_of(g * 4 * GRP, GRP), 4 * GRP), :] = dot(
+            swap, block
+        ).astype(BF)
+        return c
+
+    def weight_part(c):
+        for half in range(4):
+            lanes = (c * 8 + half * 2) * LANE
+            wg_vmem[:, lanes:lanes + 256] = dot_tn(
+                hrows[...], rows[:, lanes:lanes + 256]
             ).astype(BF)
-        return c
-
-    lax.fori_loop(0, 8, make_undo, 0)
+            for z_ in (half * 2, half * 2 + 1):
+                pltpu.make_async_copy(
+                    wg_vmem.at[:, pl.ds((c * 8 + z_) * LANE, LANE)],
+                    weight_grad.at[0, :, pl.ds(feature_block(c, z_), LANE)],
+                    o_sem,
+                ).start()
+
+    relay_back(6)
+    wait_for(hq.at[pl.ds(0, 31)], hq_r)
+    lax.fori_loop(0, 8, order_hidden, 0)
+    relay_back(7)
+    weight_part(0)
+
     for dx in range(1, 4):
         wait_for(rx.at[0], rx_r.at[dx])
     ones = jnp.ones((8, LANE), BF)
@@ -502,13 +508,15 @@
             gate_recv.at[hid], gate_recv.at[hid], gt_s, gt_r.at[d],
             (blk, (hid + d) % 4),
         )
+    weight_part(1)
     for d in range(1, 4):
         wait_for(gate_recv.at[0], gt_r.at[d])
     gate_out[...] = (gate_recv[0] + gate_recv[1]) + (gate_recv[2] + gate_recv[3])
 
     wait_for(stage.at[pl.ds(0, 3)], ex_s)
     wait_for(cols.at[0, pl.ds(0, 7)], ra_s)
-    wait_for(cols.at[pl.ds(0, 7)], rb_s)
+    wait_for(cols.at[pl.ds(0, 7), :, pl.ds(0, CHUNK)], rb_s)
+    wait_for(cols.at[0, pl.ds(0, 7), pl.ds(CHUNK, 32)], rb_s)
     wait_for(sendx.at[:, pl.ds(1, 7)], x_s)
     wait_for(hs.at[pl.ds(1, 3)], hx_s)
     wait_for(hq_send.at[pl.ds(0, 31)], hq_s)
@@ -540,8 +548,7 @@
             buf(QUAD, TOK + 16, LANE),
             buf(8, 8, CHUNK_ROWS, LANE),
             buf(8, 8 * GRP, CHUNK),
-            buf(8, 8, COL, LANE),
-            buf(2, NX, 8, COL, LANE),
+            buf(8, 8, GRP, FEATS // 2),
             buf(NX * COL, FEATS),
             buf(NX, COL, UNITS),
             buf(NX, COL, UNITS),
@@ -559,8 +566,8 @@
             pltpu.VMEM((4, 8, TOK), F32),
             dma, dma((4,)),
             dma, dma((2, 5)),
-            dma, dma((2, 5, 4)),
-            dma, dma((4,)),
+            dma, dma((2, 5, 5)),
+            dma, dma((8,)),
             dma, dma((4,)),
             dma, dma,
             dma, dma((8,)),

time: 174 us -> 178 us (1.023)
  Pallas kernels: 168 us -> 172 us
    pallas_call x1, Pallas kernels: 168 us -> 172 us  [fused(): pl.pallas_call(kernel, out_shape=(jax.ShapeDtypeStruct((SLOTS, UNITS), BF...]
where the time goes in v3:
time: 178 us; the launch traced here: 177 us
  Pallas kernels  172 us (97%)
  local copies, waits for them, and re-layouts  4.28 us (2%)
    pallas_call x1, Pallas kernels, fused(): pl.pallas_call(kernel, out_shape=(jax.ShapeDtypeStruct((SLOTS, UNITS), BF...  172 us
    unnamed x7, local copies, waits for them, and re-layouts  4.28 us

profile of v3, /device:TPU:1, one launch (start us, length us, event | category | flops | bytes accessed | tf_op | source)
XLA Modules:
  0.0 177.4 jit_solution(17301792481432138202)
XLA Ops:
  0.6 172.4 %shard_map.76 = (bf16[1024,384]{1,0:T(8,128)(2,1)}, f32[8,128]{1,0:T(8,128)}, bf16[1,384,2048]{2,1,0:T(8,128)(2,1)}) custom-call(bf16[128,512]{1,0:T(8,128)(2,1)} %og.1, bf16[1024,384]{1,0:T(8,128)(2,1)} %bitcast.7, f32[8,128]{1,0:T(8,128)} %bitcast.8, s32[8,128]{1,0:T(8,128)} %bitcast.9, bf16[1,384,2048]{2,1,0:T(8,128)(2,1)} %weight.1), custom_call_target="tpu_custom_call" | custom-call | flops 20000000000 | bytes 8000000 | tf_op jit(solution)/shard_map/pallas_call | solution.py:534
  173.1 0.0 copy-start
  173.1 2.8 %copy.11 = bf16[1,384,2048]{2,1,0:T(8,128)(2,1)} copy(bf16[1,384,2048]{2,1,0:T(8,128)(2,1)} %get-tuple-element.12) | data formatting | bytes 3145728
  175.9 0.0 copy-done
  175.9 0.0 copy-start.1
  175.9 0.9 copy.12
  176.8 0.0 copy-done.1
  176.8 0.6 copy.13
Async XLA Ops:
  173.1 2.8 %copy-start = (bf16[1024,384]{1,0:T(8,128)(2,1)S(1)}, bf16[1024,384]{1,0:T(8,128)(2,1)}, u32[]{:S(2)}) copy-start(bf16[1024,384]{1,0:T(8,128)(2,1)} %get-tuple-element.7) | copy-start | bytes 2359300
  175.9 0.9 copy-start.1

commit v4 on v2

--- a/solution.py
+++ b/solution.py
@@ -46,7 +46,7 @@
     og, hidden, gates, ids, weight,
     hidden_grad, gate_out, weight_grad,
     weighted, slot_target, slot_gate, stage, ex, cols, gsel, sendx, recvx, rows,
-    hs, hx, hq_send, hq, hrows,
+    hs, hx, hq_send, hq, pre_rows, hrows,
     rq_send, rq, r2, rx, undo, w_vmem, wg_vmem, gate_row, gate_recv,
     ex_s, ex_r, ra_s, ra_r, rb_s, rb_r, x_s, x_r,
     hx_s, hx_r, hq_s, hq_r, rq_s, rq_r, rx_s, rx_r, gt_s, gt_r, w_sem, o_sem,
@@ -84,28 +84,14 @@
         return dev(x, core * a + (1 - core) * b, core * b + (1 - core) * a, core)
 
     barrier = pltpu.get_barrier_semaphore()
-
-    def greet(device):
-        pl.semaphore_signal(barrier, inc=1, device_id=device, device_id_type=MESH)
-
-    greeted = 0
-    for step in (1, 7):
-        greet(dev_ab((pa + step) % 8, pb))
-        greet(dev_ab(pa, (pb + step) % 8))
-        greeted += 2
-    for d in range(1, 8):
-        greet(dev((x + d // 2) % 4, y, z, (core + d % 2) % 2))
-        greeted += 1
-    for d in range(1, 4):
-        greet((blk, (hid + d) % 4))
-        greeted += 1
-
-    def greet_q(d, c):
-        greet(dev_q((q + d) % 32))
-        return c
-
-    lax.fori_loop(1, 32, greet_q, 0)
-    greeted += 31
+    friends = [dev_ab((pa + step) % 8, pb) for step in (1, 7)]
+    friends += [dev_ab(pa, (pb + step) % 8) for step in (1, 7)]
+    friends += [
+        dev((x + d // 2) % 4, y, z, (core + d % 2) % 2) for d in range(1, 8)
+    ]
+    friends += [dev(x, y, (z + 4) % 8, c) for c in range(2)]
+    for friend in friends:
+        pl.semaphore_signal(barrier, inc=1, device_id=friend, device_id_type=MESH)
 
     def feature_block(c, z_):
         return (z_ % 4) * 512 + (z_ // 4) * 256 + c * 128
@@ -134,6 +120,16 @@
         stage[j, 0:TOK, :] = og[:, j * LANE:(j + 1) * LANE]
         stage[j, TOK:TOK + 16, :] = ids16
 
+    pl.semaphore_wait(barrier, len(friends))
+
+    for d in range(1, 4):
+        other = (quad + d) % 4
+        remote(
+            stage.at[other], ex.at[quad], ex_s, ex_r.at[d],
+            dev(x, y, (other // 2) * 4 + hid, other % 2),
+        )
+    ex[quad] = stage[quad]
+
     high, middle, low = (part.astype(F32) for part in thirds(gate_lanes))
     mixed = jnp.where(
         lane < 8, high,
@@ -193,19 +189,8 @@
         )
 
     select_hidden(2)
-    pl.semaphore_wait(barrier, greeted)
-
-    for d in range(1, 4):
-        other = (quad + d) % 4
-        remote(
-            stage.at[other], ex.at[quad], ex_s, ex_r.at[d],
-            dev(x, y, (other // 2) * 4 + hid, other % 2),
-        )
-    ex[quad] = stage[quad]
 
     send_hidden_x(2)
-    select_hidden(1)
-    send_hidden_x(1)
 
     for d in range(1, 4):
         wait_for(ex.at[0], ex_r.at[d])
@@ -227,9 +212,12 @@
                 ref = cols.at[pb, a, pl.ds(way * half_rows, half_rows)]
             remote(ref, ref, ra_s, ra_r.at[way, step], dev_ab((pa + sign) % 8, pb))
         if step == 1:
+            select_hidden(1)
+            send_hidden_x(1)
+        if step == 2:
             select_hidden(3)
             send_hidden_x(3)
-        if step == 2:
+        if step == 3:
             select_hidden(0)
     for way in range(2):
         wait_for(cols.at[0, 0, pl.ds(0, half_rows)], ra_r.at[way, 4])
@@ -354,6 +342,9 @@
     lax.fori_loop(0, 8, relay_hidden, 0)
     hq[q] = hq_send[q]
 
+
+    ring_wait(4)
+
     def send_hidden(d, c):
         qd = (q + d) % 32
         remote(hq_send.at[qd], hq.at[q], hq_s, hq_r, dev_q(qd))
@@ -361,7 +352,6 @@
 
     lax.fori_loop(1, 32, send_hidden, 0)
 
-    ring_wait(4)
     select((pb + 4) % 8, False)
 
     wait_for(w_vmem, w_sem)
@@ -379,13 +369,18 @@
             rows[place, FEATS // 2 + a * LANE:FEATS // 2 + (a + 1) * LANE] = recvx[
                 1, xs, a
             ]
-        hrows[place, :] = dot_nt(rows[place, :], w_vmem[...]).astype(BF)
+        pre_rows[place, :] = dot_nt(rows[place, :], w_vmem[...]).astype(BF)
+
+    def away(i):
+        first = 1 - i % 2 * 2 + (i // 2) * 2 * (1 - i % 2 * 2)
+        second = (i % 2) * 4 + ((i - 4) // 2) * 2
+        return jnp.where(i < 4, first, second) % 8
 
     def return_group(i, c):
-        ys = (y + 4 + i) % 8
+        ys = (y + away(i)) % 8
         block = jnp.concatenate(
             [
-                hrows[pl.ds(pl.multiple_of(xs * COL + ys * GRP, GRP), GRP), :]
+                pre_rows[pl.ds(pl.multiple_of(xs * COL + ys * GRP, GRP), GRP), :]
                 for xs in range(4)
             ],
             axis=0,
@@ -407,7 +402,7 @@
                 rq[q] = rq_send[qd]
         return c
 
-    lax.fori_loop(0, 8, return_group, 0)
+    lax.fori_loop(0, 4, return_group, 0)
 
     wait_for(hq.at[pl.ds(0, 31)], hq_r)
 
@@ -434,8 +429,10 @@
                     o_sem,
                 ).start()
 
+    lax.fori_loop(4, 8, return_group, 0)
+
     def relay_back(i, c):
-        dy = (4 + i) % 8
+        dy = away(i)
         g = (y - dy) % 8
 
         @pl.when(dy == 0)
@@ -548,6 +545,7 @@
             buf(NQ, GRP, UNITS),
             buf(NQ, GRP, UNITS),
             buf(NX * COL, UNITS),
+            buf(NX * COL, UNITS),
             buf(NQ, GRP, UNITS),
             buf(NQ, GRP, UNITS),
             buf(NX, COL, UNITS),

time: 174 us -> 170 us (0.977)
  Pallas kernels: 168 us -> 163 us
    pallas_call x1, Pallas kernels: 168 us -> 163 us  [fused(): pl.pallas_call(kernel, out_shape=(jax.ShapeDtypeStruct((SLOTS, UNITS), BF...]
where the time goes in v4:
time: 170 us; the launch traced here: 168 us
  Pallas kernels  163 us (96%)
  local copies, waits for them, and re-layouts  4.28 us (3%)
    pallas_call x1, Pallas kernels, fused(): pl.pallas_call(kernel, out_shape=(jax.ShapeDtypeStruct((SLOTS, UNITS), BF...  163 us
    unnamed x7, local copies, waits for them, and re-layouts  4.28 us

profile of v4, /device:TPU:1, one launch (start us, length us, event | category | flops | bytes accessed | tf_op | source)
XLA Modules:
  0.0 168.4 jit_solution(9218898736827330210)
XLA Ops:
  0.6 163.5 %shard_map.76 = (bf16[1024,384]{1,0:T(8,128)(2,1)}, f32[8,128]{1,0:T(8,128)}, bf16[1,384,2048]{2,1,0:T(8,128)(2,1)}) custom-call(bf16[128,512]{1,0:T(8,128)(2,1)} %og.1, bf16[1024,384]{1,0:T(8,128)(2,1)} %bitcast.7, f32[8,128]{1,0:T(8,128)} %bitcast.8, s32[8,128]{1,0:T(8,128)} %bitcast.9, bf16[1,384,2048]{2,1,0:T(8,128)(2,1)} %weight.1), custom_call_target="tpu_custom_call" | custom-call | flops 20000000000 | bytes 8000000 | tf_op jit(solution)/shard_map/pallas_call | solution.py:523
  164.1 0.0 copy-start
  164.1 2.8 %copy.11 = bf16[1,384,2048]{2,1,0:T(8,128)(2,1)} copy(bf16[1,384,2048]{2,1,0:T(8,128)(2,1)} %get-tuple-element.12) | data formatting | bytes 3145728
  166.9 0.0 copy-done
  166.9 0.0 copy-start.1
  166.9 0.9 copy.12
  167.8 0.0 copy-done.1
  167.8 0.6 copy.13
Async XLA Ops:
  164.1 2.8 %copy-start = (bf16[1024,384]{1,0:T(8,128)(2,1)S(1)}, bf16[1024,384]{1,0:T(8,128)(2,1)}, u32[]{:S(2)}) copy-start(bf16[1024,384]{1,0:T(8,128)(2,1)} %get-tuple-element.7) | copy-start | bytes 2359300
  166.9 0.9 copy-start.1
